TPU v7x, 32 devices: a whole 2x2x4 slice. The times are simulated.
32 devices in a mesh: chan: 16 (over z, y, core), patch: 2 (over x).
Axes of the slice: x: 2, y: 2, z: 4, core: 2. Of those that a mesh axis runs over, the one named last changes fastest.
Arguments:
- volume: bfloat16 [2, 2048, 1024], P('patch', 'chan'), may hold values from -6 to 6
- depth_kernel: bfloat16 [27, 2048], P(None, 'chan'), may hold values from -1.25 to 1.25
- mix_weight: bfloat16 [2048, 2048], P('chan'), may hold values from -0.125 to 0.125
- mix_bias: bfloat16 [2048], P('chan'), may hold values from -3 to 3
- out_grad: bfloat16 [2, 2048, 1024], P('patch', 'chan'), may hold values from -1.5 to 1.5
Outputs:
- activated: bfloat16 [2, 2048, 1024], P('patch', 'chan')
- volume_grad: bfloat16 [2, 2048, 1024], P('patch', 'chan')
- kernel_grad: float32 [27, 2048], P(None, 'chan')
- weight_grad: float32 [2048, 2048], P('chan')
- bias_grad: float32 [2048], P('chan')
All inputs are finite; a program needn't handle non-finite values.
Results may differ from a plain program's by a relative error of at most 0.011.
Values may be sent and summed in bfloat16 or wider, within the bound.
No kernel may reach another device: no remote copies, remote signals or barrier semaphores. Data moves between devices by JAX's collectives and lax.ppermute only.
A program may use at most 64 MiB of HBM per device.

v0:
```python
import jax
import jax.numpy as jnp
from jax import lax
from jax.sharding import PartitionSpec as P

DEPTH = 2
ROWS = 16
SIDE = 32


def tap_list():
    return [
        (step_z, step_y, step_x)
        for step_z in (-1, 0, 1)
        for step_y in (-1, 0, 1)
        for step_x in (-1, 0, 1)
    ]


def shifted(values, step_z, step_y, step_x):
    cell_total = DEPTH * ROWS * SIDE
    offset = step_z * ROWS * SIDE + step_y * SIDE + step_x
    margin = ROWS * SIDE + SIDE + 1
    pad_spec = [(0, 0)] * (values.ndim - 1) + [(margin, margin)]
    padded = jnp.pad(values, pad_spec)
    moved_values = lax.slice_in_dim(
        padded, margin + offset, margin + offset + cell_total, axis=values.ndim - 1
    )
    cell_index = jnp.arange(cell_total, dtype=jnp.int32)
    cell_plane = cell_index // (ROWS * SIDE)
    cell_row = cell_index // SIDE % ROWS
    cell_column = cell_index % SIDE
    inside = (cell_plane + step_z >= 0) & (cell_plane + step_z < DEPTH)
    inside = inside & (cell_row + step_y >= 0) & (cell_row + step_y < ROWS)
    inside = inside & (cell_column + step_x >= 0) & (cell_column + step_x < SIDE)
    return jnp.where(inside, moved_values, jnp.zeros_like(moved_values))


def depthwise(values, kernel, direction_sign):
    total = jnp.zeros_like(values)
    for tap_index, steps in enumerate(tap_list()):
        moved_values = shifted(
            values, direction_sign * steps[0], direction_sign * steps[1], direction_sign * steps[2]
        )
        total = total + kernel[tap_index][None, :, None] * moved_values
    return total


def folded_weight_grad(mixed_in, pre_grad):
    return jnp.einsum(
        "pos,pms->om",
        pre_grad,
        lax.all_gather(mixed_in, "chan", axis=1, tiled=True),
        preferred_element_type=jnp.float32,
    )


def body(volume, depth_kernel, mix_weight, mix_bias, out_grad):
    vol_float = volume.astype(jnp.float32)
    kernel_float = depth_kernel.astype(jnp.float32)
    mixed_in = depthwise(vol_float, kernel_float, 1).astype(jnp.bfloat16)
    pre = jnp.einsum(
        "om,pms->pos",
        mix_weight,
        lax.all_gather(mixed_in, "chan", axis=1, tiled=True),
        preferred_element_type=jnp.float32,
    )
    pre = pre + mix_bias.astype(jnp.float32)[None, :, None]
    gate = jax.nn.sigmoid(pre)
    activated = (pre * gate).astype(jnp.bfloat16)
    pre_grad = (out_grad.astype(jnp.float32) * gate * (1.0 + pre * (1.0 - gate))).astype(
        jnp.bfloat16
    )
    weight_columns = lax.all_to_all(mix_weight, "chan", split_axis=1, concat_axis=0, tiled=True)
    mixed_grad = jnp.einsum(
        "mc,pms->pcs",
        weight_columns,
        lax.all_gather(pre_grad, "chan", axis=1, tiled=True),
        preferred_element_type=jnp.float32,
    ).astype(jnp.bfloat16)
    weight_grad = folded_weight_grad(mixed_in, pre_grad)
    bias_grad = jnp.sum(pre_grad.astype(jnp.float32), axis=(0, 2))
    grad_float = mixed_grad.astype(jnp.float32)
    volume_grad = depthwise(grad_float, kernel_float, -1).astype(jnp.bfloat16)
    kernel_rows = [
        jnp.sum(grad_float * shifted(vol_float, steps[0], steps[1], steps[2]), axis=(0, 2))
        for steps in tap_list()
    ]
    kernel_grad = jnp.stack(kernel_rows, axis=0)
    weight_grad, bias_grad, kernel_grad = lax.psum((weight_grad, bias_grad, kernel_grad), "patch")
    return (activated, volume_grad, kernel_grad, weight_grad, bias_grad)


def solution(mesh):
    placed = (
        P("patch", "chan", None),
        P(None, "chan"),
        P("chan", None),
        P("chan"),
        P("patch", "chan", None),
    )
    return jax.shard_map(
        body,
        mesh=mesh,
        in_specs=placed,
        out_specs=(
            P("patch", "chan", None),
            P("patch", "chan", None),
            P(None, "chan"),
            P("chan", None),
            P("chan"),
        ),
        check_vma=False,
    )
```

profile of v0, /device:TPU:0, one launch (start us, length us, event | category | flops | bytes accessed | tf_op | source)
XLA Modules:
  0.0 187.0 jit_solution(4823021493041372597)
XLA Ops:
  7.2 0.0 all-gather.3.cloned.1.call-start
  7.4 0.7 convert_element_type.123
  8.2 1.1 copy.18
  9.4 9.7 %add_convert_fusion = bf16[1,128,1024]{1,2,0:T(8,128)(2,1)} fusion(f32[1,128,1024]{1,2,0:T(8,128)S(1)} %convert_element_type.124, f32[128]{0:T(128)S(1)} %get-tuple-element.53, f32[128]{0:T(128)S(1)} %get-tuple-element.54, f32[128]{0:T(128)S(1)} %get-tuple-element.55, f32[128]{0:T(128)S(1)} %get-tuple-element.56, f32[128]{0:T(128)S(1)} %get-tuple-element.57, ...), kind=kLoop, calls=%fused_computation.201 | loop fusion | flops 10616832 | bytes 827904 | tf_op jit(solution)/shard_map/convert_element_type | solution.py:61
  19.1 0.0 all-gather.5.cloned.1.call-start
  19.2 0.2 copy.19
  19.3 55.8 %all-gather.3.cloned.1.call-done = bf16[1,2048,1024]{1,2,0:T(8,128)(2,1)} async-done(((bf16[1,128,1024]{1,2,0:T(8,128)(2,1)}), bf16[1,2048,1024]{1,2,0:T(8,128)(2,1)}) %all-gather.3.cloned.1.call-update) | async-done | bytes 4194320 | tf_op jit(solution)/shard_map/all_gather | solution.py:65
  75.1 4.2 %convert_reduce_fusion = (f32[128]{0:T(128)S(1)}, bf16[1,128,1024]{1,2,0:T(8,128)(2,1)}, bf16[1,128,1024]{1,2,0:T(8,128)(2,1)S(1)}) fusion(bf16[1,128,1024]{1,2,0:T(8,128)(2,1)S(1)} %copy.19, f32[128]{0:T(128)S(1)} %convert_element_type.126, bf16[128,2048]{1,0:T(8,128)(2,1)S(1)} %copy-done.1, bf16[1,2048,1024]{1,2,0:T(8,128)(2,1)} %all-gather.3.cloned.1.call-done), kind=kOutput, calls=%fused_computation.170 | convolution fusion | flops 538836864 | bytes 5506048 | tf_op jit(solution)/shard_map/om,pms->pos/dot_general | solution.py:62
  79.4 0.0 all-reduce.5.cloned.1.call-start
  79.5 0.3 copy.20
  79.8 21.7 %all_to_all.19 = bf16[128,16,128]{0,2,1:T(8,128)(2,1)S(1)} all-to-all(bf16[128,16,128]{0,2,1:T(8,128)(2,1)S(1)} %bitcast.133), channel_id=1, replica_groups=mesh['chan'=16,'patch'=2] {'chan'}, dimensions={1} | all-to-all | bytes 1048576 | tf_op jit(solution)/shard_map/all_to_all | solution.py:74
  101.5 0.3 copy.21
  101.8 0.9 copy.22
  102.6 3.9 %fusion.2 = f32[128,2048]{1,0:T(8,128)} fusion(bf16[1,2048,1024]{1,2,0:T(8,128)(2,1)} %all-gather.3.cloned.1.call-done, bf16[1,128,1024]{1,2,0:T(8,128)(2,1)S(1)} %copy-done), kind=kOutput, calls=%fused_computation.54 | convolution fusion | flops 536870912 | bytes 5505024 | tf_op jit(solution)/shard_map/pos,pms->om/dot_general | solution.py:50
  106.6 30.3 %all-gather.5.cloned.1.call-done = bf16[1,2048,1024]{1,2,0:T(8,128)(2,1)} async-done(((bf16[1,128,1024]{1,2,0:T(8,128)(2,1)}), bf16[1,2048,1024]{1,2,0:T(8,128)(2,1)}) %all-gather.5.cloned.1.call-update) | async-done | bytes 4194320 | tf_op jit(solution)/shard_map/all_gather | solution.py:78
  136.9 6.7 %multiply_reduce_fusion.19 = (f32[128]{0:T(128)S(1)}, f32[128]{0:T(128)S(1)}, f32[128]{0:T(128)S(1)}, f32[128]{0:T(128)S(1)}, f32[128]{0:T(128)S(1)}, /*index=5*...) fusion(f32[1,128,1024]{1,2,0:T(8,128)S(1)} %convert_element_type.124, ...), kind=kOutput, calls=%fused_computation.190 | convolution fusion | flops 540801920 | bytes 6043136 | tf_op jit(solution)/shard_map/mc,pms->pcs/dot_general | solution.py:75
  143.6 9.2 %fusion.123 = bf16[1,128,1024]{1,2,0:T(8,128)(2,1)S(1)} fusion(f32[1,128,1024]{1,2,0:T(8,128)S(1)} %get-tuple-element.79, f32[128]{0:T(128)S(1)} %get-tuple-element.53, f32[128]{0:T(128)S(1)} %get-tuple-element.54, f32[128]{0:T(128)S(1)} %get-tuple-element.55, f32[128]{0:T(128)S(1)} %get-tuple-element.56, f32[128]{0:T(128)S(1)} %get-tuple-element.57, ...), kind=kLoop, calls=%fused_computation.161 | loop fusion | flops 10616832 | bytes 827904 | tf_op jit(solution)/shard_map/convert_element_type | solution.py:84
  152.8 0.9 copy.23
  153.7 3.0 %multiply_reduce_fusion.9 = (f32[128]{0:T(128)S(1)}, f32[128]{0:T(128)S(1)}, f32[128]{0:T(128)S(1)}, f32[128]{0:T(128)S(1)}, f32[128]{0:T(128)S(1)}, /*index=5*/...) fusion(f32[1,128,1024]{1,2,0:T(8,128)S(1)} %get-tuple-element.79, ...), kind=kLoop, calls=%fused_computation.180 | loop fusion | flops 3537792 | bytes 1062400 | tf_op jit(solution)/shard_map/reduce_sum | solution.py:86
  156.6 2.7 %multiply_reduce_fusion = (f32[128]{0:T(128)S(1)}, f32[128]{0:T(128)S(1)}, f32[128]{0:T(128)S(1)}, f32[128]{0:T(128)S(1)}, f32[128]{0:T(128)S(1)}, /*index=5*/f3...) fusion(f32[1,128,1024]{1,2,0:T(8,128)S(1)} %get-tuple-element.79, ...), kind=kLoop, calls=%fused_computation.171 | loop fusion | flops 3537792 | bytes 1062400 | tf_op jit(solution)/shard_map/reduce_sum | solution.py:86
  159.4 0.1 stack.111
  159.5 8.8 %all-reduce.2 = (f32[27,128]{1,0:T(8,128)}, f32[128]{0:T(128)}) all-reduce(f32[27,128]{1,0:T(8,128)S(1)} %stack.111, f32[128]{0:T(128)S(1)} %get-tuple-element.49), channel_id=1, replica_groups=mesh['chan'=16,'patch'=2] {'patch'}, use_global_device_ids=true, to_apply=%region_27.28 | all-reduce | flops 3584 | bytes 28672 | tf_op jit(solution)/shard_map/psum | solution.py:90
  168.3 9.9 %all-reduce.5.cloned.1.call-done = f32[128,2048]{1,0:T(8,128)} async-done(((f32[128,2048]{1,0:T(8,128)}), f32[128,2048]{1,0:T(8,128)}) %all-reduce.5.cloned.1.call-update) | async-done | bytes 1048592 | tf_op jit(solution)/shard_map/psum | solution.py:90
  178.2 2.3 %copy.25 = f32[128,2048]{1,0:T(8,128)} copy(f32[128,2048]{1,0:T(8,128)} %all-reduce.5.cloned.1.call-done) | data formatting | bytes 2097152
  (29 shorter events, 0.3 us)
Async XLA Ops:
  7.2 68.0 %all-gather.3.cloned.1.call-start = ((), (), s32[]{:S(2)}) async-start(), calls=%async_computation.1 | async-start | bytes 4456448 | tf_op jit(solution)/shard_map/all_gather | solution.py:65
  9.3 9.8 %copy-start.3 = (bf16[128]{0:T(256)(128)(2,1)S(1)}, bf16[128]{0:T(256)(128)(2,1)}, u32[]{:S(2)}) copy-start(bf16[128]{0:T(256)(128)(2,1)} %param.8) | copy-start | bytes 772
  9.3 9.9 %copy-start.2 = (bf16[1,128,1024]{2,1,0:T(8,128)(2,1)S(1)}, bf16[1,128,1024]{2,1,0:T(8,128)(2,1)}, u32[]{:S(2)}) copy-start(bf16[1,128,1024]{2,1,0:T(8,128)(2,1)} %param.9) | copy-start | bytes 786436
  9.3 65.8 %copy-start.1 = (bf16[128,2048]{1,0:T(8,128)(2,1)S(1)}, bf16[128,2048]{1,0:T(8,128)(2,1)}, u32[]{:S(2)}) copy-start(bf16[128,2048]{1,0:T(8,128)(2,1)} %param.7) | copy-start | bytes 1572868
  19.1 117.9 %all-gather.5.cloned.1.call-start = ((), (), s32[]{:S(2)}) async-start(), calls=%async_computation.2 | async-start | bytes 4456448 | tf_op jit(solution)/shard_map/all_gather | solution.py:78
  79.4 98.8 %all-reduce.5.cloned.1.call-start = ((), (), s32[]{:S(2)}) async-start(), calls=%async_computation.3 | async-start | bytes 2097152 | tf_op jit(solution)/shard_map/psum | solution.py:90
  79.8 22.9 %copy-start = (bf16[1,128,1024]{1,2,0:T(8,128)(2,1)S(1)}, bf16[1,128,1024]{1,2,0:T(8,128)(2,1)}, u32[]{:S(2)}) copy-start(bf16[1,128,1024]{1,2,0:T(8,128)(2,1)} %get-tuple-element.50) | copy-start | bytes 786436
Sparse Core Ops, SparseCore 0:
  19.2 55.9 all-gather.2
  79.5 57.3 all-gather.4
  139.8 38.3 all-reduce.4
where the time goes:
time: 187 us
  waiting for transfers between devices  96.1 us (51%)
  blocking collectives  30.5 us (16%)
  other arithmetic  25.5 us (14%)
  matrix products  14.8 us (8%)
  between operations  13.9 us (7%)
  local copies, waits for them, and re-layouts  6.03 us (3%)
    all_gather x1, waiting for transfers between devices, body(): lax.all_gather(mixed_in, 'chan', axis=1, tiled=True)  55.8 us
    all_gather x1, waiting for transfers between devices, body(): lax.all_gather(pre_grad, 'chan', axis=1, tiled=True)  30.3 us
    all_to_all x1, blocking collectives, body(): lax.all_to_all(mix_weight, 'chan', split_axis=1, concat_axis=0, tiled=True)  21.7 us
    psum x1, waiting for transfers between devices, body(): lax.psum((weight_grad, bias_grad, kernel_grad), 'patch')  9.9 us
    convert_element_type x1, other arithmetic, body(): mixed_in = depthwise(vol_float, kernel_float, 1).astype(jnp.bfloat16)  9.69 us
    convert_element_type x1, other arithmetic, body(): volume_grad = depthwise(grad_float, kernel_float, -1).astype(jnp.bfloat16)  9.2 us
    psum x1, blocking collectives, body(): lax.psum((weight_grad, bias_grad, kernel_grad), 'patch')  8.83 us
    dot_general x1, matrix products, body(): jnp.einsum('mc,pms->pcs', weight_columns, lax.all_gather(pre_grad, 'chan'...  6.67 us
  transfers between devices with their start and end apart: 3, of which 3 were waited for; matrix products, arithmetic and copies ran while one was open for 15% of the time, Pallas kernels for 0%

commit v1 on v0

v1 whole, which is shorter than its diff:
```python
import jax
import jax.numpy as jnp
from jax import lax
from jax.experimental import pallas as pl
from jax.experimental.pallas import tpu as pltpu
from jax.sharding import PartitionSpec as P

DEPTH = 2
ROWS = 16
SIDE = 32
PLANE = ROWS * SIDE
LANES = 128
VREGS = PLANE // LANES
GROUP = 8
STEP_ROWS = 16
TAPS = 27
SMALL_ROWS = 32
MIB = 1024 * 1024


def chip_at(place, chips):
    return jnp.where(place < chips // 2, 2 * place, 2 * (chips - 1 - place) + 1)


def place_of(chip, chips):
    return jnp.where(chip % 2 == 0, chip // 2, chips - 1 - chip // 2)


def lane_index():
    return lax.broadcasted_iota(jnp.int32, (GROUP, LANES), 1)


def column_shift(tiles, step, lane):
    if step == 0:
        return tiles
    inside = lane % SIDE != (SIDE - 1 if step > 0 else 0)
    return [
        jnp.where(inside, pltpu.roll(tile, (-step) % LANES, 1), 0.0) for tile in tiles
    ]


def row_shift(tiles, step, lane):
    if step == 0:
        return tiles
    turned = [pltpu.roll(tile, (-step * SIDE) % LANES, 1) for tile in tiles]
    zero = jnp.zeros_like(tiles[0])
    if step > 0:
        ahead = turned[1:] + [zero]
        return [jnp.where(lane < LANES - SIDE, now, far) for now, far in zip(turned, ahead)]
    behind = [zero] + turned[:-1]
    return [jnp.where(lane >= SIDE, now, far) for now, far in zip(turned, behind)]


def tile_list(values):
    return [values[:, LANES * at : LANES * (at + 1)] for at in range(VREGS)]


def add_tiles(left, right):
    return right if left is None else [a + b for a, b in zip(left, right)]


def scale_tiles(column, tiles):
    return [column * tile for tile in tiles]


def depthwise_kernel(vol_mine, vol_theirs, small_mine, small_theirs, out_ref, taps_ref):
    m = vol_mine.shape[0]
    core = lax.axis_index("chan") % 2
    lane = lane_index()
    same_at = pl.multiple_of(core * PLANE, PLANE)
    other_at = pl.multiple_of((1 - core) * PLANE, PLANE)
    for half, (vol_ref, small_ref) in enumerate(
        ((vol_mine, small_mine), (vol_theirs, small_theirs))
    ):
        taps_ref[half] = small_ref[...].astype(jnp.float32).T

        def group(step, carry):
            at = pl.multiple_of(step * STEP_ROWS, STEP_ROWS)
            same = vol_ref[pl.ds(at, STEP_ROWS), pl.ds(same_at, PLANE)].astype(jnp.float32)
            other = vol_ref[pl.ds(at, STEP_ROWS), pl.ds(other_at, PLANE)].astype(jnp.float32)
            taps = taps_ref[half, pl.ds(at, STEP_ROWS), :]
            parts = []
            for low in range(0, STEP_ROWS, GROUP):
                tap = taps[low : low + GROUP]
                near = tap[:, 9:18]
                far = jnp.where(core == 0, tap[:, 18:27], tap[:, 0:9])
                shifted_same = [
                    column_shift(tile_list(same[low : low + GROUP]), c, lane) for c in (-1, 0, 1)
                ]
                shifted_other = [
                    column_shift(tile_list(other[low : low + GROUP]), c, lane) for c in (-1, 0, 1)
                ]
                total = None
                for b in range(3):
                    row = None
                    for c in range(3):
                        t = 3 * b + c
                        row = add_tiles(row, scale_tiles(near[:, t : t + 1], shifted_same[c]))
                        row = add_tiles(row, scale_tiles(far[:, t : t + 1], shifted_other[c]))
                    total = add_tiles(total, row_shift(row, b - 1, lane))
                parts.append(jnp.concatenate(total, axis=1))
            out_ref[pl.ds(half * m + at, STEP_ROWS), :] = jnp.concatenate(parts, axis=0).astype(
                out_ref.dtype
            )
            return carry

        lax.fori_loop(0, m // STEP_ROWS, group, 0)


def depthwise_forward(vol_mine, vol_theirs, small_mine, small_theirs):
    m = vol_mine.shape[0]
    return pl.pallas_call(
        depthwise_kernel,
        out_shape=jax.ShapeDtypeStruct((2 * m, PLANE), jnp.bfloat16),
        in_specs=[pl.BlockSpec(memory_space=pltpu.VMEM)] * 4,
        out_specs=pl.BlockSpec(memory_space=pltpu.VMEM),
        scratch_shapes=[pltpu.VMEM((2, m, SMALL_ROWS), jnp.float32)],
        compiler_params=pltpu.CompilerParams(vmem_limit_bytes=16 * MIB),
        name="depthwise",
    )(vol_mine, vol_theirs, small_mine, small_theirs)


def mix_kernel(chips, *refs):
    w_mine, w_theirs, w_turned, small_mine, small_theirs, og_mine, og_theirs = refs[:7]
    pieces = refs[7 : 7 + 1 + chips]
    act_mine, act_theirs, grad_ref, right_ref, left_ref, all_ref = refs[8 + chips :]
    m = w_mine.shape[0]
    whole = 2 * m
    index = lax.axis_index("chan")
    core = index % 2
    place = place_of(index // 2, chips)

    def put(owner, half, rows):
        side = core if half == 0 else 1 - core
        all_ref[pl.ds(pl.multiple_of(owner * whole + side * m, m), m), :] = rows

    put(index // 2, 0, pieces[0][:m, :])
    put(index // 2, 1, pieces[0][m:, :])
    for distance in range(1, chips // 2):
        for direction in range(2):
            ref = pieces[2 * distance - 1 + direction]
            back = chips - distance if direction == 0 else distance
            owner = chip_at((place + back) % chips, chips)
            put(owner, 0, ref[:m, :])
            put(owner, 1, ref[m:, :])
    opposite = chip_at((place + chips // 2) % chips, chips)
    put(opposite, 0, pieces[chips - 1][...])
    put(opposite, 1, pieces[chips][...])
    for half, (w_ref, small_ref, og_ref, act_ref) in enumerate(
        (
            (w_mine, small_mine, og_mine, act_mine),
            (w_theirs, small_theirs, og_theirs, act_theirs),
        )
    ):
        bias = small_ref[...].astype(jnp.float32).T[:, TAPS : TAPS + 1]
        pre = jnp.dot(w_ref[...], all_ref[...], preferred_element_type=jnp.float32) + bias
        gate = jax.nn.sigmoid(pre)
        act_ref[...] = (pre * gate).astype(act_ref.dtype)
        grad = og_ref[...].astype(jnp.float32) * gate * (1.0 + pre * (1.0 - gate))
        grad_ref[half * m : (half + 1) * m, :] = grad.astype(grad_ref.dtype)
    block = w_turned[pl.ds(pl.multiple_of(opposite * whole, whole), whole), :]
    first = jnp.dot(block, grad_ref[...], preferred_element_type=jnp.float32)
    right_ref[...] = first[:m].astype(right_ref.dtype)
    left_ref[...] = first[m:].astype(left_ref.dtype)


def mix(chips, w_mine, w_theirs, w_turned, small_mine, small_theirs, og_mine, og_theirs, pieces):
    m = w_mine.shape[0]
    half = jax.ShapeDtypeStruct((m, PLANE), jnp.bfloat16)
    both = jax.ShapeDtypeStruct((2 * m, PLANE), jnp.bfloat16)
    full = jax.ShapeDtypeStruct((2 * m * chips, PLANE), jnp.bfloat16)
    return pl.pallas_call(
        lambda *refs: mix_kernel(chips, *refs),
        out_shape=(half, half, both, half, half, full),
        in_specs=[pl.BlockSpec(memory_space=pltpu.VMEM)] * (7 + len(pieces)),
        out_specs=[pl.BlockSpec(memory_space=pltpu.VMEM)] * 6,
        compiler_params=pltpu.CompilerParams(vmem_limit_bytes=32 * MIB),
        name="mix",
    )(w_mine, w_theirs, w_turned, small_mine, small_theirs, og_mine, og_theirs, *pieces)


def backward_kernel(grad_ref, far_ref, vol_ref, small_ref, out_ref, taps_grad_ref, taps_ref, planes, sums):
    m = vol_ref.shape[0]
    core = lax.axis_index("chan") % 2
    lane = lane_index()
    taps_ref[...] = small_ref[...].astype(jnp.float32).T
    planes[core] = grad_ref[pl.ds(pl.multiple_of(core * m, m), m), :]
    planes[1 - core] = far_ref[...]

    def group(step, carry):
        at = pl.multiple_of(step * STEP_ROWS, STEP_ROWS)
        rows = pl.ds(at, STEP_ROWS)
        vol = [
            vol_ref[rows, z * PLANE : (z + 1) * PLANE].astype(jnp.float32) for z in range(DEPTH)
        ]
        grad = [planes[z, rows, :].astype(jnp.float32) for z in range(DEPTH)]
        taps = taps_ref[rows, :]
        out_parts = [[], []]
        sum_parts = []
        for low in range(0, STEP_ROWS, GROUP):
            tap = taps[low : low + GROUP]
            moved_vol = [
                [column_shift(tile_list(vol[z][low : low + GROUP]), c, lane) for c in (-1, 0, 1)]
                for z in range(DEPTH)
            ]
            moved_grad = [
                [row_shift(tile_list(grad[z][low : low + GROUP]), -b, lane) for b in (-1, 0, 1)]
                for z in range(DEPTH)
            ]
            for z in range(DEPTH):
                total = None
                for c in range(3):
                    column = None
                    for a in (-1, 0, 1):
                        if not 0 <= z - a < DEPTH:
                            continue
                        for b in range(3):
                            t = 9 * (a + 1) + 3 * b + c
                            column = add_tiles(
                                column, scale_tiles(tap[:, t : t + 1], moved_grad[z - a][b])
                            )
                    total = add_tiles(total, column_shift(column, -(c - 1), lane))
                out_parts[z].append(jnp.concatenate(total, axis=1))
            collected = jnp.zeros((GROUP, LANES), jnp.float32)
            for a in (-1, 0, 1):
                for b in range(3):
                    for c in range(3):
                        t = 9 * (a + 1) + 3 * b + c
                        acc = None
                        for z in range(DEPTH):
                            if not 0 <= z + a < DEPTH:
                                continue
                            for left, right in zip(moved_grad[z][b], moved_vol[z + a][c]):
                                acc = left * right if acc is None else acc + left * right
                        collected = jnp.where(
                            lane == t, jnp.sum(acc, axis=1, keepdims=True), collected
                        )
            sum_parts.append(collected)
        for z in range(DEPTH):
            out_ref[rows, z * PLANE : (z + 1) * PLANE] = jnp.concatenate(
                out_parts[z], axis=0
            ).astype(out_ref.dtype)
        sums[rows, :] = jnp.concatenate(sum_parts, axis=0)
        return carry

    lax.fori_loop(0, m // STEP_ROWS, group, 0)
    taps_grad_ref[...] = sums[...].T[:SMALL_ROWS, :]


def depthwise_backward(grad, far, volume, small):
    m = volume.shape[0]
    return pl.pallas_call(
        backward_kernel,
        out_shape=(
            jax.ShapeDtypeStruct((m, DEPTH * PLANE), jnp.bfloat16),
            jax.ShapeDtypeStruct((SMALL_ROWS, m), jnp.float32),
        ),
        in_specs=[pl.BlockSpec(memory_space=pltpu.VMEM)] * 4,
        out_specs=[pl.BlockSpec(memory_space=pltpu.VMEM)] * 2,
        scratch_shapes=[
            pltpu.VMEM((m, SMALL_ROWS), jnp.float32),
            pltpu.VMEM((DEPTH, m, PLANE), jnp.bfloat16),
            pltpu.VMEM((m, LANES), jnp.float32),
        ],
        compiler_params=pltpu.CompilerParams(vmem_limit_bytes=16 * MIB),
        name="depthwise_back",
    )(grad, far, volume, small)


def body(volume, depth_kernel, mix_weight, mix_bias, out_grad):
    n = lax.axis_size("chan")
    patches = lax.axis_size("patch")
    chips = n // 2
    half_ring = chips // 2
    index = lax.axis_index("chan")
    core = index % 2
    chip = index // 2
    place = place_of(chip, chips)
    m = mix_weight.shape[0]
    whole = 2 * m

    ring = [2 * k if k < half_ring else 2 * (chips - 1 - k) + 1 for k in range(chips)]
    to_core = [(i, i ^ 1) for i in range(n)]
    to_right = [
        (2 * ring[k] + c, 2 * ring[(k + 1) % chips] + c) for k in range(chips) for c in range(2)
    ]
    to_left = [(target, source) for source, target in to_right]

    def swap(values):
        return lax.ppermute(values, "chan", to_core)

    def over_patches(values, kind):
        if patches != 2:
            return lax.psum(values, "patch")
        kept = values
        if kind != values.dtype:
            kept = lax.reduce_precision(values, 8, 7)
        came = lax.ppermute(kept.astype(kind), "patch", [(0, 1), (1, 0)])
        return kept + came.astype(values.dtype)

    vol_mine = volume[0]
    small_mine = jnp.concatenate(
        [
            depth_kernel,
            mix_bias[None, :],
            jnp.zeros((SMALL_ROWS - TAPS - 1, m), jnp.bfloat16),
        ],
        axis=0,
    )
    vol_theirs = swap(vol_mine)
    small_theirs = swap(small_mine)
    grad_planes = out_grad[0]
    og_mine = lax.dynamic_slice(grad_planes, (0, core * PLANE), (m, PLANE))
    og_theirs = swap(lax.dynamic_slice(grad_planes, (0, (1 - core) * PLANE), (m, PLANE)))
    w_theirs = swap(mix_weight)
    w_turned = jnp.concatenate([mix_weight, w_theirs], axis=0).T

    mixed_in = depthwise_forward(vol_mine, vol_theirs, small_mine, small_theirs)

    pieces = [mixed_in]
    rightward = leftward = mixed_in
    for step in range(1, half_ring):
        rightward = lax.ppermute(rightward, "chan", to_right)
        leftward = lax.ppermute(leftward, "chan", to_left)
        pieces += [rightward, leftward]
    pieces.append(lax.ppermute(rightward[:m], "chan", to_right))
    pieces.append(lax.ppermute(leftward[m:], "chan", to_left))

    act_mine, act_theirs, pre_grad, rightward, leftward, all_mixed = mix(
        chips, mix_weight, w_theirs, w_turned, small_mine, small_theirs, og_mine, og_theirs, pieces
    )

    rightward = lax.ppermute(rightward, "chan", to_right)
    leftward = lax.ppermute(leftward, "chan", to_left)
    shares = jnp.dot(w_turned, pre_grad, preferred_element_type=jnp.float32)

    def share(distance):
        owner = chip_at((place + distance) % chips, chips)
        return lax.dynamic_slice(shares, (owner * whole, 0), (whole, PLANE))

    for step in range(1, half_ring):
        ahead = share(half_ring - step)
        behind = share(chips - (half_ring - step))
        came_right = rightward.astype(jnp.float32)
        came_left = leftward.astype(jnp.float32)
        if step == 1:
            came_right = jnp.pad(came_right, ((0, m), (0, 0)))
            came_left = jnp.pad(came_left, ((m, 0), (0, 0)))
        rightward = lax.ppermute((ahead + came_right).astype(jnp.bfloat16), "chan", to_right)
        leftward = lax.ppermute((behind + came_left).astype(jnp.bfloat16), "chan", to_left)
    mixed_grad = (
        share(0) + rightward.astype(jnp.float32) + leftward.astype(jnp.float32)
    ).astype(jnp.bfloat16)

    weight_part = lax.dot_general(
        pre_grad, all_mixed, (((1,), (1,)), ((), ())), preferred_element_type=jnp.float32
    )
    weight_sum = weight_part[:m] + swap(weight_part[m:].astype(jnp.bfloat16)).astype(jnp.float32)
    weight_grad = over_patches(weight_sum, jnp.bfloat16)
    bias_part = jnp.sum(pre_grad.astype(jnp.float32), axis=1)
    bias_sum = bias_part[:m] + swap(bias_part[m:])
    act_far = swap(act_theirs)
    activated = jnp.where(
        core == 0,
        jnp.concatenate([act_mine, act_far], axis=1),
        jnp.concatenate([act_far, act_mine], axis=1),
    )

    far = swap(lax.dynamic_slice(mixed_grad, ((1 - core) * m, 0), (m, PLANE)))
    volume_grad, small_grad = depthwise_backward(mixed_grad, far, vol_mine, small_mine)
    small_grad = over_patches(
        jnp.concatenate([small_grad[:TAPS], bias_sum[None, :], small_grad[TAPS + 1 :]], axis=0),
        jnp.float32,
    )
    return (
        activated[None],
        volume_grad[None],
        small_grad[:TAPS],
        weight_grad,
        small_grad[TAPS],
    )


def solution(mesh):
    placed = (
        P("patch", "chan", None),
        P(None, "chan"),
        P("chan", None),
        P("chan"),
        P("patch", "chan", None),
    )
    return jax.shard_map(
        body,
        mesh=mesh,
        in_specs=placed,
        out_specs=(
            P("patch", "chan", None),
            P("patch", "chan", None),
            P(None, "chan"),
            P("chan", None),
            P("chan"),
        ),
        check_vma=False,
    )
```

time: 187 us -> 108 us (0.58)
  waiting for transfers between devices: 96.1 us -> 43.7 us
  blocking collectives: 30.5 us -> 0 us
  starting transfers between devices: 0.12 us -> 21 us
  other arithmetic: 25.5 us -> 11.5 us
  between operations: 13.9 us -> 1.12 us
  matrix products: 14.8 us -> 2.48 us
  local copies, waits for them, and re-layouts: 6.03 us -> 16.7 us
  Pallas kernels: 0 us -> 10.6 us
    all_gather x2 -> x0, waiting for transfers between devices: 86.2 us -> none  [the longest x1 55.8 us: body(): lax.all_gather(mixed_in, 'chan', axis=1, tiled=True)]
    ppermute x0 -> x26, waiting for transfers between devices: none -> 43.7 us  [the longest x4 13.8 us: body(): rightward = lax.ppermute(rightward, 'chan', to_right)]
    all_to_all x1 -> x0, blocking collectives: 21.7 us -> none  [body(): lax.all_to_all(mix_weight, 'chan', split_axis=1, concat_axis=0, tiled=True)]
    ppermute x0 -> x26, starting transfers between devices: none -> 21 us  [the longest x4 7.69 us: body(): rightward = lax.ppermute(rightward, 'chan', to_right)]
    dot_general x3 -> x2, matrix products: 14.8 us -> 2.48 us  [the longest x1 1.74 us: body(): shares = jnp.dot(w_turned, pre_grad, preferred_element_type=jnp.float32)]
    convert_element_type x5 -> x7, other arithmetic: 19.6 us -> 7.47 us  [the longest x3 3.2 us: body(): (ahead + came_right).astype(jnp.bfloat16)]
    pallas_call x0 -> x3, Pallas kernels: none -> 10.6 us  [the longest x1 5.18 us: depthwise_backward(): pl.pallas_call(backward_kernel, out_shape=(jax.ShapeDtypeStruct((m, DEPTH...]
    psum x1 -> x0, waiting for transfers between devices: 9.9 us -> none  [body(): lax.psum((weight_grad, bias_grad, kernel_grad), 'patch')]
  transfers between devices with their start and end apart: 3 -> 26, of which waited for: 3 -> 16; matrix products, arithmetic and copies ran while one was open for 15% -> 14% of each run, Pallas kernels for 0% -> 5%
where the time goes in v1:
time: 108 us; the launch traced here: 107 us
  waiting for transfers between devices  43.7 us (40%)
  starting transfers between devices  21 us (19%)
  local copies, waits for them, and re-layouts  16.7 us (15%)
  other arithmetic  11.5 us (11%)
  Pallas kernels  10.6 us (10%)
  matrix products  2.48 us (2%)
  between operations  1.12 us (1%)
    ppermute x4, waiting for transfers between devices, body(): rightward = lax.ppermute(rightward, 'chan', to_right)  13.8 us
    unnamed x61, local copies, waits for them, and re-layouts  13.7 us
    ppermute x3, waiting for transfers between devices, body(): lax.ppermute((behind + came_left).astype(jnp.bfloat16), 'chan', to_left)  13.4 us
    ppermute x4, starting transfers between devices, body(): rightward = lax.ppermute(rightward, 'chan', to_right)  7.69 us
    ppermute x4, waiting for transfers between devices, body(): leftward = lax.ppermute(leftward, 'chan', to_left)  6.49 us
    ppermute x3, starting transfers between devices, body(): lax.ppermute((ahead + came_right).astype(jnp.bfloat16), 'chan', to_right)  5.29 us
    pallas_call x1, Pallas kernels, depthwise_backward(): pl.pallas_call(backward_kernel, out_shape=(jax.ShapeDtypeStruct((m, DEPTH...  5.18 us
    ppermute x3, waiting for transfers between devices, body(): lax.ppermute((ahead + came_right).astype(jnp.bfloat16), 'chan', to_right)  5.08 us
  transfers between devices with their start and end apart: 26, of which 16 were waited for; matrix products, arithmetic and copies ran while one was open for 14% of the time, Pallas kernels for 5%

profile of v1, /device:TPU:0, one launch (start us, length us, event | category | flops | bytes accessed | tf_op | source)
XLA Modules:
  0.0 107.1 jit_solution(931602135894083400)
XLA Ops:
  4.2 4.1 %depthwise.1.refs_7_ = bf16[256,512]{1,0:T(8,128)(2,1)S(1)} custom-call(bf16[128,1024]{1,0:T(8,128)(2,1)S(1)} %bitcast.21, bf16[128,1024]{1,0:T(8,128)(2,1)S(1)} %collective-permute-done.3.vol_theirs, bf16[32,128]{1,0:T(8,128)(2,1)S(1)} %maximum_maximum_fusion.small_mine.refs_3_.small_ref, bf16[32,128]{1,0:T(8,128)(2,1)S(1)} %collective-permute-done.1.small_theirs.refs_4_), custom_call_target="tpu_custom_call" | custom-call | tf_op jit(solution)/shard_map/depthwise/pallas_call | solution.py:112
  8.3 2.8 %collective-permute-start.4 = (bf16[256,512]{1,0:T(8,128)(2,1)S(1)}, bf16[256,512]{1,0:T(8,128)(2,1)S(1)}, u32[]{:S(2)}, u32[]{:S(2)}) collective-permute-start(bf16[256,512]{1,0:T(8,128)(2,1)S(1)} %depthwise.1.refs_7_), channel_id=1, source_target_pairs={{0,8},{2,10},{8,16},{10,18},{16,24},{18,26},{24,28},{26,30},{28,20... | collective-permute-start | bytes 786440 | tf_op jit(solution)/shard_map/ppermute | solution.py:323
  12.6 5.3 %collective-permute-done.4.refs_8_ = bf16[256,512]{1,0:T(8,128)(2,1)S(1)} collective-permute-done((bf16[256,512]{1,0:T(8,128)(2,1)S(1)}, bf16[256,512]{1,0:T(8,128)(2,1)S(1)}, u32[]{:S(2)}, u32[]{:S(2)}) %collective-permute-start.4) | collective-permute-done | bytes 262176 | tf_op jit(solution)/shard_map/ppermute | solution.py:323
  17.9 1.8 %collective-permute-start.6 = (bf16[256,512]{1,0:T(8,128)(2,1)S(1)}, bf16[256,512]{1,0:T(8,128)(2,1)S(1)}, u32[]{:S(2)}, u32[]{:S(2)}) collective-permute-start(bf16[256,512]{1,0:T(8,128)(2,1)S(1)} %collective-permute-done.4.refs_8_), channel_id=1, source_target_pairs={{0,8},{2,10},{8,16},{10,18},{16,24},{18,26},{24,28},{26,30},{28,20... | collective-permute-start | bytes 786440 | tf_op jit(solution)/shard_map/ppermute | solution.py:323
  21.3 4.6 %collective-permute-done.6.refs_10_ = bf16[256,512]{1,0:T(8,128)(2,1)S(1)} collective-permute-done((bf16[256,512]{1,0:T(8,128)(2,1)S(1)}, bf16[256,512]{1,0:T(8,128)(2,1)S(1)}, u32[]{:S(2)}, u32[]{:S(2)}) %collective-permute-start.6) | collective-permute-done | bytes 262176 | tf_op jit(solution)/shard_map/ppermute | solution.py:323
  25.9 1.5 %collective-permute-start.8 = (bf16[256,512]{1,0:T(8,128)(2,1)S(1)}, bf16[256,512]{1,0:T(8,128)(2,1)S(1)}, u32[]{:S(2)}, u32[]{:S(2)}) collective-permute-start(bf16[256,512]{1,0:T(8,128)(2,1)S(1)} %collective-permute-done.6.refs_10_), channel_id=1, source_target_pairs={{0,8},{2,10},{8,16},{10,18},{16,24},{18,26},{24,28},{26,30},{28,20... | collective-permute-start | bytes 786440 | tf_op jit(solution)/shard_map/ppermute | solution.py:323
  30.9 2.3 %collective-permute-done.8.refs_12_ = bf16[256,512]{1,0:T(8,128)(2,1)S(1)} collective-permute-done((bf16[256,512]{1,0:T(8,128)(2,1)S(1)}, bf16[256,512]{1,0:T(8,128)(2,1)S(1)}, u32[]{:S(2)}, u32[]{:S(2)}) %collective-permute-start.8) | collective-permute-done | bytes 262176 | tf_op jit(solution)/shard_map/ppermute | solution.py:323
  48.3 1.6 %collective-permute-start.13 = (bf16[128,512]{1,0:T(8,128)(2,1)S(1)}, bf16[128,512]{1,0:T(8,128)(2,1)S(1)}, u32[]{:S(2)}, u32[]{:S(2)}) collective-permute-start(bf16[128,512]{1,0:T(8,128)(2,1)S(1)} %get-tuple-element.16), channel_id=1, source_target_pairs={{0,8},{2,10},{8,16},{10,18},{16,24},{18,26},{24,28},{26,30},{28,20... | collective-permute-start | bytes 393224 | tf_op jit(solution)/shard_map/ppermute | solution.py:333
  49.9 1.7 %fusion.1 = f32[2048,512]{1,0:T(8,128)S(1)} fusion(bf16[256,512]{1,0:T(8,128)(2,1)S(1)} %get-tuple-element.15, bf16[128,2048]{0,1:T(8,128)(2,1)} %collective-permute-done, bf16[128,2048]{0,1:T(8,128)(2,1)S(1)} %copy-done.28), kind=kOutput, calls=%fused_computation.5 | convolution fusion | flops 538968064 | bytes 5505024 | tf_op jit(solution)/shard_map/dot_general | solution.py:335
  51.7 1.6 %collective-permute-done.13 = bf16[128,512]{1,0:T(8,128)(2,1)S(1)} collective-permute-done((bf16[128,512]{1,0:T(8,128)(2,1)S(1)}, bf16[128,512]{1,0:T(8,128)(2,1)S(1)}, u32[]{:S(2)}, u32[]{:S(2)}) %collective-permute-start.13) | collective-permute-done | bytes 131104 | tf_op jit(solution)/shard_map/ppermute | solution.py:333
  53.7 1.6 %collective-permute-start.14 = (bf16[256,512]{1,0:T(8,128)(2,1)S(1)}, bf16[256,512]{1,0:T(8,128)(2,1)S(1)}, u32[]{:S(2)}, u32[]{:S(2)}) collective-permute-start(bf16[256,512]{1,0:T(8,128)(2,1)S(1)} %add_convert_fusion.6), channel_id=1, source_target_pairs={{0,8},{2,10},{8,16},{10,18},{16,24},{18,26},{24,28},{26,30},{28,20... | collective-permute-start | bytes 786440 | tf_op jit(solution)/shard_map/ppermute | solution.py:349
  55.4 5.1 %collective-permute-done.14 = bf16[256,512]{1,0:T(8,128)(2,1)S(1)} collective-permute-done((bf16[256,512]{1,0:T(8,128)(2,1)S(1)}, bf16[256,512]{1,0:T(8,128)(2,1)S(1)}, u32[]{:S(2)}, u32[]{:S(2)}) %collective-permute-start.14) | collective-permute-done | bytes 262176 | tf_op jit(solution)/shard_map/ppermute | solution.py:349
  61.5 1.6 %collective-permute-start.15 = (bf16[256,512]{1,0:T(8,128)(2,1)S(1)}, bf16[256,512]{1,0:T(8,128)(2,1)S(1)}, u32[]{:S(2)}, u32[]{:S(2)}) collective-permute-start(bf16[256,512]{1,0:T(8,128)(2,1)S(1)} %add_convert_fusion.5), channel_id=1, source_target_pairs={{0,8},{2,10},{8,16},{10,18},{16,24},{18,26},{24,28},{26,30},{28,20... | collective-permute-start | bytes 786440 | tf_op jit(solution)/shard_map/ppermute | solution.py:349
  63.6 6.0 %collective-permute-done.17 = bf16[128,512]{1,0:T(8,128)(2,1)S(1)} collective-permute-done((bf16[128,512]{1,0:T(8,128)(2,1)}, bf16[128,512]{1,0:T(8,128)(2,1)S(1)}, u32[]{:S(2)}, u32[]{:S(2)}) %collective-permute-start.17) | collective-permute-done | bytes 131104 | tf_op jit(solution)/shard_map/ppermute | solution.py:334
  69.6 2.0 %add_convert_fusion.4 = (bf16[256,512]{1,0:T(8,128)(2,1)}, bf16[256,512]{1,0:T(8,128)(2,1)S(1)}) fusion(bf16[256,512]{1,0:T(8,128)(2,1)S(1)} %collective-permute-done.15, f32[2048,512]{1,0:T(8,128)} %copy-done.24, s32[]{:T(128)S(6)} %select_n.130, bf16[128,512]{1,0:T(8,128)(2,1)S(1)} %collective-permute-done.17, s32[]{:T(128)S(6)} %select_n.145), kind=kLoop, calls=%fused_computation.13 | loop fusion | flops 786432 | bytes 1966088 | tf_op jit(solution)/shard_map/convert_element_type | solution.py:349
  72.4 1.3 %copy-done.25 = f32[256,2048]{1,0:T(8,128)} copy-done((f32[256,2048]{1,0:T(8,128)}, f32[256,2048]{1,0:T(8,128)S(1)}, u32[]{:S(2)}) %copy-start.25) | copy-done | bytes 2097176
  73.9 4.8 %collective-permute-done.18 = bf16[256,512]{1,0:T(8,128)(2,1)S(1)} collective-permute-done((bf16[256,512]{1,0:T(8,128)(2,1)S(1)}, bf16[256,512]{1,0:T(8,128)(2,1)S(1)}, u32[]{:S(2)}, u32[]{:S(2)}) %collective-permute-start.18) | collective-permute-done | bytes 262176 | tf_op jit(solution)/shard_map/ppermute | solution.py:350
  78.7 1.8 %add_convert_fusion.2 = bf16[256,512]{1,0:T(8,128)(2,1)} fusion(bf16[256,512]{1,0:T(8,128)(2,1)S(1)} %collective-permute-done.18, f32[2048,512]{1,0:T(8,128)} %copy-done.24, s32[]{:T(128)S(6)} %select_n.142), kind=kLoop, calls=%fused_computation.11 | loop fusion | flops 393216 | bytes 1048580 | tf_op jit(solution)/shard_map/convert_element_type | solution.py:350
  81.3 2.0 %collective-permute-start.16 = (bf16[256,512]{1,0:T(8,128)(2,1)}, bf16[256,512]{1,0:T(8,128)(2,1)S(1)}, u32[]{:S(2)}, u32[]{:S(2)}) collective-permute-start(bf16[256,512]{1,0:T(8,128)(2,1)} %get-tuple-element.21), channel_id=1, source_target_pairs={{0,8},{2,10},{8,16},{10,18},{16,24},{18,26},{24,28},{26,30},{28,20... | collective-permute-start | bytes 786440 | tf_op jit(solution)/shard_map/ppermute | solution.py:349
  83.3 4.0 %collective-permute-done.19 = bf16[256,512]{1,0:T(8,128)(2,1)} collective-permute-done((bf16[256,512]{1,0:T(8,128)(2,1)}, bf16[256,512]{1,0:T(8,128)(2,1)}, u32[]{:S(2)}, u32[]{:S(2)}) %collective-permute-start.19) | collective-permute-done | bytes 262176 | tf_op jit(solution)/shard_map/ppermute | solution.py:350
  88.7 1.6 %collective-permute-start.25 = (bf16[128,2048]{1,0:T(8,128)(2,1)S(1)}, bf16[128,2048]{1,0:T(8,128)(2,1)S(1)}, u32[]{:S(2)}, u32[]{:S(2)}) collective-permute-start(bf16[128,2048]{1,0:T(8,128)(2,1)S(1)} %fusion.3), channel_id=1, source_target_pairs={{0,1},{1,0},{2,3},{3,2},{4,5},{5,4},{6,7},{7,6},{8,9},{9,8},{10,11... | collective-permute-start | bytes 1572872 | tf_op jit(solution)/shard_map/ppermute | solution.py:298
  90.2 4.6 %collective-permute-done.20 = bf16[256,512]{1,0:T(8,128)(2,1)S(1)} collective-permute-done((bf16[256,512]{1,0:T(8,128)(2,1)S(1)}, bf16[256,512]{1,0:T(8,128)(2,1)S(1)}, u32[]{:S(2)}, u32[]{:S(2)}) %collective-permute-start.20) | collective-permute-done | bytes 262176 | tf_op jit(solution)/shard_map/ppermute | solution.py:350
  97.5 5.2 %depthwise_back.1 = (bf16[128,1024]{1,0:T(8,128)(2,1)}, f32[32,128]{1,0:T(8,128)S(1)}) custom-call(bf16[256,512]{1,0:T(8,128)(2,1)S(1)} %add_convert_fusion.grad_ref, bf16[128,512]{1,0:T(8,128)(2,1)S(1)} %collective-permute-done.21.far_ref, bf16[128,1024]{1,0:T(8,128)(2,1)S(1)} %bitcast.22, bf16[32,128]{1,0:T(8,128)(2,1)S(1)} %maximum_maximum_fusion.small_mine.refs_3_.small_ref), custom_call_target="tpu_custom_call" | custom-call | tf_op jit(solution)/shard_map/depthwise_back/pallas_call | solution.py:252
  102.7 1.6 %collective-permute-start.23 = (f32[32,128]{1,0:T(8,128)S(1)}, f32[32,128]{1,0:T(8,128)S(1)}, u32[]{:S(2)}, u32[]{:S(2)}) collective-permute-start(f32[32,128]{1,0:T(8,128)S(1)} %pad_maximum_fusion.2), channel_id=1, source_target_pairs={{0,1},{1,0},{2,3},{3,2},{4,5},{5,4},{6,7},{7,6},{8,9},{9,8},{10,11... | collective-permute-start | bytes 49160 | tf_op jit(solution)/shard_map/ppermute | solution.py:298
  (120 shorter events, 35.3 us)
Async XLA Ops:
  0.6 2.6 %collective-permute-start.3 = (bf16[128,1024]{1,0:T(8,128)(2,1)}, bf16[128,1024]{1,0:T(8,128)(2,1)S(1)}, u32[]{:S(2)}, u32[]{:S(2)}) collective-permute-start(bf16[128,1024]{1,0:T(8,128)(2,1)} %bitcast.20), channel_id=1, source_target_pairs={{0,2},{2,0},{4,6},{6,4},{8,10},{10,8},{12,14},{14,12},{16,18},{18,... | collective-permute-start | bytes 786440 | tf_op jit(solution)/shard_map/ppermute | solution.py:290
  8.3 9.5 %collective-permute-start.4 = (bf16[256,512]{1,0:T(8,128)(2,1)S(1)}, bf16[256,512]{1,0:T(8,128)(2,1)S(1)}, u32[]{:S(2)}, u32[]{:S(2)}) collective-permute-start(bf16[256,512]{1,0:T(8,128)(2,1)S(1)} %depthwise.1.refs_7_), channel_id=1, source_target_pairs={{0,8},{2,10},{8,16},{10,18},{16,24},{18,26},{24,28},{26,30},{28,20... | collective-permute-start | bytes 786440 | tf_op jit(solution)/shard_map/ppermute | solution.py:323
  11.1 9.3 %collective-permute-start.5 = (bf16[256,512]{1,0:T(8,128)(2,1)S(1)}, bf16[256,512]{1,0:T(8,128)(2,1)S(1)}, u32[]{:S(2)}, u32[]{:S(2)}) collective-permute-start(bf16[256,512]{1,0:T(8,128)(2,1)S(1)} %depthwise.1.refs_7_), channel_id=1, source_target_pairs={{8,0},{10,2},{16,8},{18,10},{24,16},{26,18},{28,24},{30,26},{20,28... | collective-permute-start | bytes 786440 | tf_op jit(solution)/shard_map/ppermute | solution.py:324
  12.4 17.1 %collective-permute-start = (bf16[128,2048]{0,1:T(8,128)(2,1)S(1)}, bf16[128,2048]{0,1:T(8,128)(2,1)}, u32[]{:S(2)}, u32[]{:S(2)}) collective-permute-start(bf16[128,2048]{0,1:T(8,128)(2,1)S(1)} %copy.10), channel_id=1, source_target_pairs={{0,2},{2,0},{4,6},{6,4},{8,10},{10,8},{12,14},{14,12},{16,18},{18,... | collective-permute-start | bytes 1572872 | tf_op jit(solution)/shard_map/ppermute | solution.py:290
  17.9 8.1 %collective-permute-start.6 = (bf16[256,512]{1,0:T(8,128)(2,1)S(1)}, bf16[256,512]{1,0:T(8,128)(2,1)S(1)}, u32[]{:S(2)}, u32[]{:S(2)}) collective-permute-start(bf16[256,512]{1,0:T(8,128)(2,1)S(1)} %collective-permute-done.4.refs_8_), channel_id=1, source_target_pairs={{0,8},{2,10},{8,16},{10,18},{16,24},{18,26},{24,28},{26,30},{28,20... | collective-permute-start | bytes 786440 | tf_op jit(solution)/shard_map/ppermute | solution.py:323
  20.4 7.5 %collective-permute-start.7 = (bf16[256,512]{1,0:T(8,128)(2,1)S(1)}, bf16[256,512]{1,0:T(8,128)(2,1)S(1)}, u32[]{:S(2)}, u32[]{:S(2)}) collective-permute-start(bf16[256,512]{1,0:T(8,128)(2,1)S(1)} %collective-permute-done.5.refs_9_), channel_id=1, source_target_pairs={{8,0},{10,2},{16,8},{18,10},{24,16},{26,18},{28,24},{30,26},{20,28... | collective-permute-start | bytes 786440 | tf_op jit(solution)/shard_map/ppermute | solution.py:324
  25.9 7.2 %collective-permute-start.8 = (bf16[256,512]{1,0:T(8,128)(2,1)S(1)}, bf16[256,512]{1,0:T(8,128)(2,1)S(1)}, u32[]{:S(2)}, u32[]{:S(2)}) collective-permute-start(bf16[256,512]{1,0:T(8,128)(2,1)S(1)} %collective-permute-done.6.refs_10_), channel_id=1, source_target_pairs={{0,8},{2,10},{8,16},{10,18},{16,24},{18,26},{24,28},{26,30},{28,20... | collective-permute-start | bytes 786440 | tf_op jit(solution)/shard_map/ppermute | solution.py:323
  27.8 6.5 %collective-permute-start.9 = (bf16[256,512]{1,0:T(8,128)(2,1)S(1)}, bf16[256,512]{1,0:T(8,128)(2,1)S(1)}, u32[]{:S(2)}, u32[]{:S(2)}) collective-permute-start(bf16[256,512]{1,0:T(8,128)(2,1)S(1)} %collective-permute-done.7.refs_11_), channel_id=1, source_target_pairs={{8,0},{10,2},{16,8},{18,10},{24,16},{26,18},{28,24},{30,26},{20,28... | collective-permute-start | bytes 786440 | tf_op jit(solution)/shard_map/ppermute | solution.py:324
  29.4 7.1 %collective-permute-start.2 = (bf16[128,512]{1,0:T(8,128)(2,1)S(1)}, bf16[128,512]{1,0:T(8,128)(2,1)S(1)}, u32[]{:S(2)}, u32[]{:S(2)}) collective-permute-start(bf16[128,512]{1,0:T(8,128)(2,1)S(1)} %get-tuple-element.23), channel_id=1, source_target_pairs={{0,2},{2,0},{4,6},{6,4},{8,10},{10,8},{12,14},{14,12},{16,18},{18,... | collective-permute-start | bytes 393224 | tf_op jit(solution)/shard_map/ppermute | solution.py:290
  33.2 5.0 %collective-permute-start.10 = (bf16[128,512]{1,0:T(8,128)(2,1)S(1)}, bf16[128,512]{1,0:T(8,128)(2,1)S(1)}, u32[]{:S(2)}, u32[]{:S(2)}) collective-permute-start(bf16[128,512]{1,0:T(8,128)(2,1)S(1)} %slice.41), channel_id=1, source_target_pairs={{0,8},{2,10},{8,16},{10,18},{16,24},{18,26},{24,28},{26,30},{28,20... | collective-permute-start | bytes 393224 | tf_op jit(solution)/shard_map/ppermute | solution.py:326
  34.4 5.0 %collective-permute-start.11 = (bf16[128,512]{1,0:T(8,128)(2,1)S(1)}, bf16[128,512]{1,0:T(8,128)(2,1)S(1)}, u32[]{:S(2)}, u32[]{:S(2)}) collective-permute-start(bf16[128,512]{1,0:T(8,128)(2,1)S(1)} %slice.42), channel_id=1, source_target_pairs={{8,0},{10,2},{16,8},{18,10},{24,16},{26,18},{28,24},{30,26},{20,28... | collective-permute-start | bytes 393224 | tf_op jit(solution)/shard_map/ppermute | solution.py:327
  48.3 5.0 %collective-permute-start.13 = (bf16[128,512]{1,0:T(8,128)(2,1)S(1)}, bf16[128,512]{1,0:T(8,128)(2,1)S(1)}, u32[]{:S(2)}, u32[]{:S(2)}) collective-permute-start(bf16[128,512]{1,0:T(8,128)(2,1)S(1)} %get-tuple-element.16), channel_id=1, source_target_pairs={{0,8},{2,10},{8,16},{10,18},{16,24},{18,26},{24,28},{26,30},{28,20... | collective-permute-start | bytes 393224 | tf_op jit(solution)/shard_map/ppermute | solution.py:333
  53.7 6.7 %collective-permute-start.14 = (bf16[256,512]{1,0:T(8,128)(2,1)S(1)}, bf16[256,512]{1,0:T(8,128)(2,1)S(1)}, u32[]{:S(2)}, u32[]{:S(2)}) collective-permute-start(bf16[256,512]{1,0:T(8,128)(2,1)S(1)} %add_convert_fusion.6), channel_id=1, source_target_pairs={{0,8},{2,10},{8,16},{10,18},{16,24},{18,26},{24,28},{26,30},{28,20... | collective-permute-start | bytes 786440 | tf_op jit(solution)/shard_map/ppermute | solution.py:349
  61.5 8.1 %collective-permute-start.15 = (bf16[256,512]{1,0:T(8,128)(2,1)S(1)}, bf16[256,512]{1,0:T(8,128)(2,1)S(1)}, u32[]{:S(2)}, u32[]{:S(2)}) collective-permute-start(bf16[256,512]{1,0:T(8,128)(2,1)S(1)} %add_convert_fusion.5), channel_id=1, source_target_pairs={{0,8},{2,10},{8,16},{10,18},{16,24},{18,26},{24,28},{26,30},{28,20... | collective-permute-start | bytes 786440 | tf_op jit(solution)/shard_map/ppermute | solution.py:349
  63.2 6.4 %collective-permute-start.17 = (bf16[128,512]{1,0:T(8,128)(2,1)}, bf16[128,512]{1,0:T(8,128)(2,1)S(1)}, u32[]{:S(2)}, u32[]{:S(2)}) collective-permute-start(bf16[128,512]{1,0:T(8,128)(2,1)} %copy-done.23), channel_id=1, source_target_pairs={{8,0},{10,2},{16,8},{18,10},{24,16},{26,18},{28,24},{30,26},{20,28... | collective-permute-start | bytes 393224 | tf_op jit(solution)/shard_map/ppermute | solution.py:334
  71.7 7.1 %collective-permute-start.18 = (bf16[256,512]{1,0:T(8,128)(2,1)S(1)}, bf16[256,512]{1,0:T(8,128)(2,1)S(1)}, u32[]{:S(2)}, u32[]{:S(2)}) collective-permute-start(bf16[256,512]{1,0:T(8,128)(2,1)S(1)} %get-tuple-element.22), channel_id=1, source_target_pairs={{8,0},{10,2},{16,8},{18,10},{24,16},{26,18},{28,24},{30,26},{20,28... | collective-permute-start | bytes 786440 | tf_op jit(solution)/shard_map/ppermute | solution.py:350
  73.8 14.7 %collective-permute-start.24 = (bf16[128,2048]{1,0:T(8,128)(2,1)S(1)}, bf16[128,2048]{1,0:T(8,128)(2,1)S(1)}, u32[]{:S(2)}, u32[]{:S(2)}) collective-permute-start(bf16[128,2048]{1,0:T(8,128)(2,1)S(1)} %slice.57), channel_id=1, source_target_pairs={{0,2},{2,0},{4,6},{6,4},{8,10},{10,8},{12,14},{14,12},{16,18},{18,... | collective-permute-start | bytes 1572872 | tf_op jit(solution)/shard_map/ppermute | solution.py:290
  80.6 6.7 %collective-permute-start.19 = (bf16[256,512]{1,0:T(8,128)(2,1)}, bf16[256,512]{1,0:T(8,128)(2,1)}, u32[]{:S(2)}, u32[]{:S(2)}) collective-permute-start(bf16[256,512]{1,0:T(8,128)(2,1)} %add_convert_fusion.2), channel_id=1, source_target_pairs={{8,0},{10,2},{16,8},{18,10},{24,16},{26,18},{28,24},{30,26},{20,28... | collective-permute-start | bytes 786440 | tf_op jit(solution)/shard_map/ppermute | solution.py:350
  80.7 15.5 %collective-permute-start.22 = (f32[128]{0:T(128)S(1)}, f32[128]{0:T(128)S(1)}, u32[]{:S(2)}, u32[]{:S(2)}) collective-permute-start(f32[128]{0:T(128)S(1)} %slice.35), channel_id=1, source_target_pairs={{0,2},{2,0},{4,6},{6,4},{8,10},{10,8},{12,14},{14,12},{16,18},{18,... | collective-permute-start | bytes 1544 | tf_op jit(solution)/shard_map/ppermute | solution.py:290
  80.8 15.4 %collective-permute-start.12 = (bf16[128,512]{1,0:T(8,128)(2,1)S(1)}, bf16[128,512]{1,0:T(8,128)(2,1)S(1)}, u32[]{:S(2)}, u32[]{:S(2)}) collective-permute-start(bf16[128,512]{1,0:T(8,128)(2,1)S(1)} %copy-done.22), channel_id=1, source_target_pairs={{0,2},{2,0},{4,6},{6,4},{8,10},{10,8},{12,14},{14,12},{16,18},{18,... | collective-permute-start | bytes 393224 | tf_op jit(solution)/shard_map/ppermute | solution.py:290
  81.3 9.0 %collective-permute-start.16 = (bf16[256,512]{1,0:T(8,128)(2,1)}, bf16[256,512]{1,0:T(8,128)(2,1)S(1)}, u32[]{:S(2)}, u32[]{:S(2)}) collective-permute-start(bf16[256,512]{1,0:T(8,128)(2,1)} %get-tuple-element.21), channel_id=1, source_target_pairs={{0,8},{2,10},{8,16},{10,18},{16,24},{18,26},{24,28},{26,30},{28,20... | collective-permute-start | bytes 786440 | tf_op jit(solution)/shard_map/ppermute | solution.py:349
  88.5 6.4 %collective-permute-start.20 = (bf16[256,512]{1,0:T(8,128)(2,1)S(1)}, bf16[256,512]{1,0:T(8,128)(2,1)S(1)}, u32[]{:S(2)}, u32[]{:S(2)}) collective-permute-start(bf16[256,512]{1,0:T(8,128)(2,1)S(1)} %add_convert_fusion.1), channel_id=1, source_target_pairs={{8,0},{10,2},{16,8},{18,10},{24,16},{26,18},{28,24},{30,26},{20,28... | collective-permute-start | bytes 786440 | tf_op jit(solution)/shard_map/ppermute | solution.py:350
  88.7 15.6 %collective-permute-start.25 = (bf16[128,2048]{1,0:T(8,128)(2,1)S(1)}, bf16[128,2048]{1,0:T(8,128)(2,1)S(1)}, u32[]{:S(2)}, u32[]{:S(2)}) collective-permute-start(bf16[128,2048]{1,0:T(8,128)(2,1)S(1)} %fusion.3), channel_id=1, source_target_pairs={{0,1},{1,0},{2,3},{3,2},{4,5},{5,4},{6,7},{7,6},{8,9},{9,8},{10,11... | collective-permute-start | bytes 1572872 | tf_op jit(solution)/shard_map/ppermute | solution.py:298
  102.7 3.8 %collective-permute-start.23 = (f32[32,128]{1,0:T(8,128)S(1)}, f32[32,128]{1,0:T(8,128)S(1)}, u32[]{:S(2)}, u32[]{:S(2)}) collective-permute-start(f32[32,128]{1,0:T(8,128)S(1)} %pad_maximum_fusion.2), channel_id=1, source_target_pairs={{0,1},{1,0},{2,3},{3,2},{4,5},{5,4},{6,7},{7,6},{8,9},{9,8},{10,11... | collective-permute-start | bytes 49160 | tf_op jit(solution)/shard_map/ppermute | solution.py:298
  (32 other events, 165.6 us)
